TPU v7x, 32 devices: a whole 2x2x4 slice. The times are simulated.
32 devices in a mesh: row: 4 (over z), col: 2 (over x), rep: 4 (over y, core).
Axes of the slice: x: 2, y: 2, z: 4, core: 2. Of those that a mesh axis runs over, the one named last changes fastest.
Arguments:
- tokens_in: bfloat16 [1024, 12288], P(('col', 'rep'), 'row'), may hold values from -6 to 6
- w_up: bfloat16 [12288, 24576], P('row', ('col', 'rep')), may hold values from -0.0546875 to 0.0546875
- w_down: bfloat16 [24576, 12288], P(('col', 'rep'), 'row'), may hold values from -0.0390625 to 0.0390625
- grad_out: bfloat16 [1024, 12288], P(('col', 'rep'), 'row'), may hold values from -6 to 6
Outputs:
- output: bfloat16 [1024, 12288], P(('col', 'rep'), 'row')
- grad_tokens: bfloat16 [1024, 12288], P(('col', 'rep'), 'row')
- grad_w_up: bfloat16 [12288, 24576], P('row', ('col', 'rep'))
- grad_w_down: bfloat16 [24576, 12288], P(('col', 'rep'), 'row')
All inputs are finite; a program needn't handle non-finite values.
Results may differ from a plain program's by a relative error of at most 0.0049.
Values may be sent and summed in bfloat16 or wider, within the bound.
A program may use at most 192 MiB of HBM per device.

v0:
```python
import jax
import jax.numpy as jnp
from jax import lax
from jax.sharding import PartitionSpec as P


def product(left_rows, weight, transposed):
    if transposed:
        return lax.dot_general(
            left_rows, weight, (((1,), (1,)), ((), ())), preferred_element_type=jnp.float32
        )
    return jnp.dot(left_rows, weight, preferred_element_type=jnp.float32)


def row_term(left_rows, weight, transposed):

    def term(first_row, row_total):
        return product(left_rows, weight, transposed)

    return term


def share_sum(left_rows, weight, transposed):
    row_count = left_rows.shape[0] // lax.axis_size("row")
    return lax.psum_scatter(
        row_term(left_rows, weight, transposed)(jnp.int32(0), lax.axis_size("row") * row_count),
        "row",
        scatter_dimension=0,
        tiled=True,
    )


def gather_rows(shares):
    return lax.all_gather(shares, "row", axis=0, tiled=True)


def output_sum(left_rows, weight, transposed):
    term = row_term(left_rows, weight, transposed)
    row_count = left_rows.shape[0] // (lax.axis_size("col") * lax.axis_size("rep"))
    summed = lax.psum_scatter(
        term(jnp.int32(0), lax.axis_size(("col", "rep")) * row_count),
        ("col", "rep"),
        scatter_dimension=0,
        tiled=True,
    )
    return summed.astype(jnp.bfloat16)


def gelu_parts(hidden):
    normal_cdf = 0.5 * (1.0 + lax.erf(hidden * 0.7071067811865476))
    density = jnp.exp(-0.5 * hidden * hidden) * 0.3989422804014327
    return (normal_cdf, density)


def on_device(tokens_in, w_up, w_down, grad_out):
    tokens_all, grad_out_all = (
        lax.all_gather(tokens_in, ("col", "rep"), axis=0, tiled=True),
        lax.all_gather(grad_out, ("col", "rep"), axis=0, tiled=True),
    )
    token_scale = tokens_all.shape[0] ** (-0.5)
    hidden = share_sum(tokens_all, w_up, False)
    normal_cdf, density = gelu_parts(hidden)
    activ_all = gather_rows((hidden * normal_cdf).astype(jnp.bfloat16))
    output = output_sum(activ_all, w_down, False)
    grad_activ = share_sum(grad_out_all, w_down, True)
    grad_all = gather_rows((grad_activ * (normal_cdf + hidden * density)).astype(jnp.bfloat16))
    contract_rows = (((0,), (0,)), ((), ()))
    grad_w_down = (
        lax.dot_general(activ_all, grad_out_all, contract_rows, preferred_element_type=jnp.float32)
        * token_scale
    ).astype(jnp.bfloat16)
    grad_w_up = (
        lax.dot_general(tokens_all, grad_all, contract_rows, preferred_element_type=jnp.float32)
        * token_scale
    ).astype(jnp.bfloat16)
    grad_tokens = output_sum(grad_all, w_up, True)
    return (output, grad_tokens, grad_w_up, grad_w_down)


def solution(mesh):
    return jax.shard_map(
        on_device,
        mesh=mesh,
        in_specs=(
            P(("col", "rep"), "row"),
            P("row", ("col", "rep")),
            P(("col", "rep"), "row"),
            P(("col", "rep"), "row"),
        ),
        out_specs=(
            P(("col", "rep"), "row"),
            P(("col", "rep"), "row"),
            P("row", ("col", "rep")),
            P(("col", "rep"), "row"),
        ),
        check_vma=False,
    )
```

profile of v0, /device:TPU:0, one launch (start us, length us, event | category | flops | bytes accessed | tf_op | source)
XLA Modules:
  0.0 972.3 jit_solution(518723547616188551)
XLA Ops:
  7.2 0.0 all-gather.9.cloned.1.call-start
  7.2 0.7 all-gather.9.cloned.1.call-update
  7.9 0.0 all-gather.5.cloned.1.call-start
  7.9 0.7 all-gather.5.cloned.1.call-update
  8.6 0.0 reduce-scatter.9.cloned.1.call-start
  8.7 49.4 %all-gather.9.cloned.1.call-done = bf16[1024,3072]{1,0:T(8,128)(2,1)} async-done(((bf16[128,3072]{1,0:T(8,128)(2,1)}), bf16[1024,3072]{1,0:T(8,128)(2,1)}) %all-gather.9.cloned.1.call-update) | async-done | bytes 6291472 | tf_op jit(solution)/shard_map/all_gather | solution.py:58
  58.1 26.2 %fusion.9 = f32[1024,3072]{1,0:T(8,128)} fusion(bf16[1024,3072]{1,0:T(8,128)(2,1)} %all-gather.9.cloned.1.call-done, bf16[3072,3072]{1,0:T(8,128)(2,1)} %param.6), kind=kOutput, calls=%fused_computation.14 | convolution fusion | flops 19327352832 | bytes 37748736 | tf_op jit(solution)/shard_map/dot_general | solution.py:9
  84.3 0.0 reduce-scatter.9.cloned.1.call-update
  84.4 0.0 reduce-scatter.5.cloned.1.call-start
  84.4 21.2 %all-gather.5.cloned.1.call-done = bf16[1024,3072]{1,0:T(8,128)(2,1)} async-done(((bf16[128,3072]{1,0:T(8,128)(2,1)}), bf16[1024,3072]{1,0:T(8,128)(2,1)}) %all-gather.5.cloned.1.call-update) | async-done | bytes 6291472 | tf_op jit(solution)/shard_map/all_gather | solution.py:57
  105.6 26.1 %fusion.7 = f32[1024,3072]{1,0:T(8,128)} fusion(bf16[1024,3072]{1,0:T(8,128)(2,1)} %all-gather.5.cloned.1.call-done, bf16[3072,3072]{1,0:T(8,128)(2,1)} %param.5), kind=kOutput, calls=%fused_computation.12 | convolution fusion | flops 19327352832 | bytes 37748736 | tf_op jit(solution)/shard_map/dot_general | solution.py:12
  131.6 0.0 reduce-scatter.5.cloned.1.call-update
  131.7 0.0 all-gather.7.cloned.1.call-start
  131.7 188.7 %reduce-scatter.9.cloned.1.call-done = f32[256,3072]{1,0:T(8,128)} async-done(((f32[1024,3072]{1,0:T(8,128)}), f32[256,3072]{1,0:T(8,128)}) %reduce-scatter.9.cloned.1.call-update) | async-done | bytes 3145744 | tf_op jit(solution)/shard_map/reduce_scatter | solution.py:25
  320.4 215.7 %reduce-scatter.5.cloned.1.call-done = f32[256,3072]{1,0:T(8,128)} async-done(((f32[1024,3072]{1,0:T(8,128)}), f32[256,3072]{1,0:T(8,128)}) %reduce-scatter.5.cloned.1.call-update) | async-done | bytes 3145744 | tf_op jit(solution)/shard_map/reduce_scatter | solution.py:25
  536.1 4.7 fusion.6
  540.8 0.0 all-gather.7.cloned.1.call-update
  540.8 0.0 all-gather.11.cloned.1.call-start
  540.9 0.5 all-gather.11.cloned.1.call-update
  541.4 0.2 reduce-scatter.7.cloned.1.call-start
  541.6 115.8 %all-gather.7.cloned.1.call-done = bf16[1024,3072]{1,0:T(8,128)(2,1)} async-done(((bf16[256,3072]{1,0:T(8,128)(2,1)}), bf16[1024,3072]{1,0:T(8,128)(2,1)}) %all-gather.7.cloned.1.call-update) | async-done | bytes 6291472 | tf_op jit(solution)/shard_map/all_gather | solution.py:34
  657.4 26.2 %fusion.8 = f32[1024,3072]{1,0:T(8,128)} fusion(bf16[1024,3072]{1,0:T(8,128)(2,1)} %all-gather.7.cloned.1.call-done, bf16[3072,3072]{1,0:T(8,128)(2,1)} %param.6), kind=kOutput, calls=%fused_computation.13 | convolution fusion | flops 19327352832 | bytes 37748736 | tf_op jit(solution)/shard_map/dot_general | solution.py:12
  683.6 0.0 reduce-scatter.7.cloned.1.call-update
  683.6 0.0 reduce-scatter.11.cloned.1.call-start
  683.6 89.4 %all-gather.11.cloned.1.call-done = bf16[1024,3072]{1,0:T(8,128)(2,1)} async-done(((bf16[256,3072]{1,0:T(8,128)(2,1)}), bf16[1024,3072]{1,0:T(8,128)(2,1)}) %all-gather.11.cloned.1.call-update) | async-done | bytes 6291472 | tf_op jit(solution)/shard_map/all_gather | solution.py:34
  773.0 26.2 %fusion.10 = f32[1024,3072]{1,0:T(8,128)} fusion(bf16[1024,3072]{1,0:T(8,128)(2,1)} %all-gather.11.cloned.1.call-done, bf16[3072,3072]{1,0:T(8,128)(2,1)} %param.5), kind=kOutput, calls=%fused_computation.15 | convolution fusion | flops 19327352832 | bytes 37748736 | tf_op jit(solution)/shard_map/dot_general | solution.py:9
  799.3 26.5 %fusion = bf16[3072,3072]{0,1:T(8,128)(2,1)} fusion(bf16[1024,3072]{1,0:T(8,128)(2,1)} %all-gather.11.cloned.1.call-done, bf16[1024,3072]{1,0:T(8,128)(2,1)} %all-gather.5.cloned.1.call-done), kind=kOutput, calls=%fused_computation.2 | convolution fusion | flops 19346227200 | bytes 31457280 | tf_op jit(solution)/shard_map/dot_general | solution.py:73
  825.8 24.7 %copy.8 = bf16[3072,3072]{1,0:T(8,128)(2,1)} copy(bf16[3072,3072]{0,1:T(8,128)(2,1)} %fusion) | data formatting | bytes 37748736
  850.5 26.9 %multiply_convert_fusion = bf16[3072,3072]{1,0:T(8,128)(2,1)} fusion(bf16[1024,3072]{1,0:T(8,128)(2,1)} %all-gather.7.cloned.1.call-done, bf16[1024,3072]{1,0:T(8,128)(2,1)} %all-gather.9.cloned.1.call-done), kind=kOutput, calls=%fused_computation | convolution fusion | flops 19346227200 | bytes 31457280 | tf_op jit(solution)/shard_map/dot_general | solution.py:69
  877.4 2.4 convert_element_type.22
  879.8 83.3 %reduce-scatter.11.cloned.1.call-done = f32[128,3072]{1,0:T(8,128)} async-done(((f32[1024,3072]{1,0:T(8,128)}), f32[128,3072]{1,0:T(8,128)}) %reduce-scatter.11.cloned.1.call-update) | async-done | bytes 1572880 | tf_op jit(solution)/shard_map/reduce_scatter | solution.py:40
  963.1 2.4 convert_element_type.24
  (2 shorter events, 0.0 us)
Async XLA Ops:
  7.2 51.0 %all-gather.9.cloned.1.call-start = ((), (), s32[]{:S(2)}) async-start(), calls=%async_computation.8 | async-start | bytes 7077888 | tf_op jit(solution)/shard_map/all_gather | solution.py:58
  7.9 97.7 %all-gather.5.cloned.1.call-start = ((), (), s32[]{:S(2)}) async-start(), calls=%async_computation.4 | async-start | bytes 7077888 | tf_op jit(solution)/shard_map/all_gather | solution.py:57
  8.6 311.7 %reduce-scatter.9.cloned.1.call-start = ((), (), s32[]{:S(2)}) async-start(), calls=%async_computation.9 | async-start | bytes 15728640 | tf_op jit(solution)/shard_map/reduce_scatter | solution.py:25
  84.4 451.8 %reduce-scatter.5.cloned.1.call-start = ((), (), s32[]{:S(2)}) async-start(), calls=%async_computation.5 | async-start | bytes 15728640 | tf_op jit(solution)/shard_map/reduce_scatter | solution.py:25
  131.7 525.7 %all-gather.7.cloned.1.call-start = ((), (), s32[]{:S(2)}) async-start(), calls=%async_computation.6 | async-start | bytes 7864320 | tf_op jit(solution)/shard_map/all_gather | solution.py:34
  540.8 232.2 %all-gather.11.cloned.1.call-start = ((), (), s32[]{:S(2)}) async-start(), calls=%async_computation.10 | async-start | bytes 7864320 | tf_op jit(solution)/shard_map/all_gather | solution.py:34
  541.4 336.0 %reduce-scatter.7.cloned.1.call-start = ((), (), s32[]{:S(2)}) async-start(), calls=%async_computation.7 | async-start | bytes 14155776 | tf_op jit(solution)/shard_map/reduce_scatter | solution.py:40
  683.6 279.5 %reduce-scatter.11.cloned.1.call-start = ((), (), s32[]{:S(2)}) async-start(), calls=%async_computation.11 | async-start | bytes 14155776 | tf_op jit(solution)/shard_map/reduce_scatter | solution.py:40
Sparse Core Ops, SparseCore 0:
  9.9 48.2 all-gather.8
  60.0 45.5 all-gather.4
  108.5 211.8 reduce-scatter.8
  323.2 212.8 reduce-scatter.4
  541.0 116.3 all-gather.6
  659.4 113.5 all-gather.10
  776.5 90.6 reduce-scatter.6
  870.7 92.3 reduce-scatter.10
where the time goes:
time: 973 us; the launch traced here: 972 us
  waiting for transfers between devices  765 us (79%)
  matrix products  158 us (16%)
  local copies, waits for them, and re-layouts  24.7 us (3%)
  between operations  14.1 us (1%)
    reduce_scatter x2, waiting for transfers between devices, share_sum(): lax.psum_scatter(row_term(left_rows, weight, transposed)(jnp.int32(0), la...  404 us
    all_gather x2, waiting for transfers between devices, gather_rows(): return lax.all_gather(shares, 'row', axis=0, tiled=True)  205 us
    reduce_scatter x2, waiting for transfers between devices, output_sum(): lax.psum_scatter(term(jnp.int32(0), lax.axis_size(('col', 'rep')) * row_c...  83.3 us
    dot_general x2, matrix products, product(): lax.dot_general(left_rows, weight, (((1,), (1,)), ((), ())), preferred_el...  52.4 us
    dot_general x2, matrix products, product(): return jnp.dot(left_rows, weight, preferred_element_type=jnp.float32)  52.2 us
    all_gather x1, waiting for transfers between devices, on_device(): lax.all_gather(grad_out, ('col', 'rep'), axis=0, tiled=True)  49.4 us
    dot_general x1, matrix products, on_device(): lax.dot_general(activ_all, grad_out_all, contract_rows, preferred_element...  26.9 us
    dot_general x1, matrix products, on_device(): lax.dot_general(tokens_all, grad_all, contract_rows, preferred_element_ty...  26.5 us
  transfers between devices with their start and end apart: 8, of which 7 were waited for; matrix products, arithmetic and copies ran while one was open for 19% of the time, Pallas kernels for 0%

commit v1 on v0

v1 whole, which is shorter than its diff:
```python
import jax
import jax.numpy as jnp
from jax import lax
from jax.sharding import PartitionSpec as P

TOKEN_AXES = ("col", "rep")
BF16 = jnp.bfloat16


def product(left_rows, weight, transposed):
    weight_dim = 1 if transposed else 0
    return lax.dot_general(
        left_rows, weight, (((1,), (weight_dim,)), ((), ())), preferred_element_type=jnp.float32
    )


def swap(block, distance):
    count = lax.axis_size(TOKEN_AXES)
    return lax.ppermute(block, TOKEN_AXES, [(i, i ^ distance) for i in range(count)])


def gather_chunks(block):
    chunks = []
    for distance in range(0, lax.axis_size(TOKEN_AXES), 2):
        first = block if distance == 0 else swap(block, distance)
        chunks.append(jnp.concatenate([first, swap(first, 1)], axis=0))
    return chunks


def pick(options, index):
    chosen = options[-1]
    for at in range(len(options) - 2, -1, -1):
        chosen = jnp.where(index == at, options[at], chosen)
    return chosen


def run_line(terms, finish):
    size, at, count = lax.axis_size("row"), lax.axis_index("row"), len(terms)
    half = size // 2
    lower = at < half
    depth = jnp.minimum(at, size - 1 - at)
    nothing = jnp.zeros(terms[0].shape, BF16)
    from_end, outward, finals = nothing, nothing, []
    for tick in range(count + size - 2):
        own = [terms[min(max(tick - k, 0), count - 1)] for k in range(half)]
        inward = pick(own, depth) + from_end.astype(jnp.float32)
        sent = inward.astype(BF16)
        busy = [i for i in range(size - 1) if 0 <= tick - i < count]
        right = lax.ppermute(
            jnp.where(lower, sent, outward), "row", [(i, i + 1) for i in busy]
        )
        left = lax.ppermute(
            jnp.where(lower, outward, sent), "row", [(size - 1 - i, size - 2 - i) for i in busy]
        )
        from_end = jnp.where(lower, right, left)
        outward = jnp.where(lower, left, right)
        term_at = tick - (half - 1)
        if 0 <= term_at < count:
            finished = finish(term_at, inward + outward.astype(jnp.float32))
            outward = jnp.where(depth == half - 1, finished, outward)
        finals.append(outward)
    return [
        pick([finals[u + size - 2 - k] for k in range(half)], depth) for u in range(count)
    ]


def sum_chunks(terms):
    total = None
    for at, term in enumerate(terms):
        rows = term.shape[0] // 2
        pair = term[:rows] + swap(term[rows:], 1)
        if at > 0:
            pair = swap(pair.astype(BF16), 2 * at).astype(jnp.float32)
        total = pair if total is None else total + pair
    return total.astype(BF16)


def gelu_parts(hidden):
    normal_cdf = 0.5 * (1.0 + lax.erf(hidden * 0.7071067811865476))
    density = jnp.exp(-0.5 * hidden * hidden) * 0.3989422804014327
    return (normal_cdf, density)


def on_device(tokens_in, w_up, w_down, grad_out):
    token_chunks = gather_chunks(tokens_in)
    grad_chunks = gather_chunks(grad_out)
    token_scale = (tokens_in.shape[0] * lax.axis_size(TOKEN_AXES)) ** (-0.5)
    chunk_count, rows = len(token_chunks), tokens_in.shape[0]
    terms = [product(chunk, w_up, False) for chunk in token_chunks]
    terms += [product(chunk, w_down, True) for chunk in grad_chunks]

    def run_half(first_row):
        slopes = []

        def finish(term_at, total):
            if term_at >= chunk_count:
                return (total * slopes[term_at - chunk_count]).astype(BF16)
            normal_cdf, density = gelu_parts(total)
            slopes.append(normal_cdf + total * density)
            return (total * normal_cdf).astype(BF16)

        return run_line([term[first_row : first_row + rows] for term in terms], finish)

    finals = [
        jnp.concatenate(pair, axis=0) for pair in zip(run_half(0), run_half(rows))
    ]
    activs, grads = finals[:chunk_count], finals[chunk_count:]
    output = sum_chunks([product(activ, w_down, False) for activ in activs])
    grad_tokens = sum_chunks([product(grad, w_up, True) for grad in grads])
    contract_rows = (((0,), (0,)), ((), ()))

    def weight_grad(left, right):
        summed = lax.dot_general(
            jnp.concatenate(left, axis=0),
            jnp.concatenate(right, axis=0),
            contract_rows,
            preferred_element_type=jnp.float32,
        )
        return (summed * token_scale).astype(BF16)

    grad_w_down = weight_grad(activs, grad_chunks)
    grad_w_up = weight_grad(token_chunks, grads)
    return (output, grad_tokens, grad_w_up, grad_w_down)


def solution(mesh):
    return jax.shard_map(
        on_device,
        mesh=mesh,
        in_specs=(
            P(("col", "rep"), "row"),
            P("row", ("col", "rep")),
            P(("col", "rep"), "row"),
            P(("col", "rep"), "row"),
        ),
        out_specs=(
            P(("col", "rep"), "row"),
            P(("col", "rep"), "row"),
            P("row", ("col", "rep")),
            P(("col", "rep"), "row"),
        ),
        check_vma=False,
    )
```

time: 973 us -> 663 us (0.68)
  waiting for transfers between devices: 765 us -> 178 us
  starting transfers between devices: 0.5 us -> 120 us
  other arithmetic: 9.5 us -> 97.5 us
  matrix products: 158 us -> 208 us
  local copies, waits for them, and re-layouts: 24.7 us -> 47.6 us
  between operations: 14.1 us -> 2.41 us
    reduce_scatter x4 -> x0, waiting for transfers between devices: 488 us -> none  [the longest x2 404 us: share_sum(): lax.psum_scatter(row_term(left_rows, weight, transposed)(jnp.int32(0), la...]
    all_gather x4 -> x0, waiting for transfers between devices: 276 us -> none  [the longest x2 205 us: gather_rows(): return lax.all_gather(shares, 'row', axis=0, tiled=True)]
    ppermute x0 -> x68, waiting for transfers between devices: none -> 178 us  [the longest x20 89.8 us: run_line(): lax.ppermute(jnp.where(lower, outward, sent), 'row', [(size - 1 - i, size...]
    ppermute x0 -> x68, starting transfers between devices: none -> 120 us  [the longest x20 75.6 us: run_line(): lax.ppermute(jnp.where(lower, sent, outward), 'row', [(i, i + 1) for i in...]
    dot_general x6 -> x18, matrix products: 158 us -> 208 us  [the longest x16 154 us: product(): lax.dot_general(left_rows, weight, (((1,), (weight_dim,)), ((), ())), pre...]
    select_n x0 -> x28, other arithmetic: none -> 42.5 us  [the longest x12 28.3 us: run_line(): jnp.where(lower, sent, outward)]
    unnamed x0 -> x15, other arithmetic: none -> 34.5 us
    unnamed x1 -> x198, local copies, waits for them, and re-layouts: 24.7 us -> 34 us
  transfers between devices with their start and end apart: 8 -> 68, of which waited for: 7 -> 23; matrix products, arithmetic and copies ran while one was open for 19% -> 51% of each run, Pallas kernels for 0% -> 0%
where the time goes in v1:
time: 663 us; the launch traced here: 653 us
  matrix products  208 us (31%)
  waiting for transfers between devices  178 us (27%)
  starting transfers between devices  120 us (18%)
  other arithmetic  97.5 us (15%)
  local copies, waits for them, and re-layouts  47.6 us (7%)
    dot_general x16, matrix products, product(): lax.dot_general(left_rows, weight, (((1,), (weight_dim,)), ((), ())), pre...  154 us
    ppermute x20, waiting for transfers between devices, run_line(): lax.ppermute(jnp.where(lower, outward, sent), 'row', [(size - 1 - i, size...  89.8 us
    ppermute x20, starting transfers between devices, run_line(): lax.ppermute(jnp.where(lower, sent, outward), 'row', [(i, i + 1) for i in...  75.6 us
    dot_general x2, matrix products, weight_grad(): lax.dot_general(jnp.concatenate(left, axis=0), jnp.concatenate(right, axi...  53.5 us
    ppermute x20, waiting for transfers between devices, run_line(): lax.ppermute(jnp.where(lower, sent, outward), 'row', [(i, i + 1) for i in...  53.2 us
    ppermute x28, waiting for transfers between devices, swap(): lax.ppermute(block, TOKEN_AXES, [(i, i ^ distance) for i in range(count)])  35.4 us
    unnamed x15, other arithmetic  34.5 us
    unnamed x198, local copies, waits for them, and re-layouts  34 us
  transfers between devices with their start and end apart: 68, of which 23 were waited for; matrix products, arithmetic and copies ran while one was open for 51% of the time, Pallas kernels for 0%

profile of v1, /device:TPU:0, one launch (start us, length us, event | category | flops | bytes accessed | tf_op | source)
XLA Modules:
  0.0 653.2 jit_solution(17349743749535688719)
XLA Ops:
  9.9 10.8 %fusion.86 = f32[256,3072]{1,0:T(8,128)} fusion(bf16[3072,3072]{1,0:T(8,128)(2,1)} %param.6, bf16[128,3072]{1,0:T(8,128)(2,1)S(1)} %collective-permute-done.26, bf16[128,3072]{1,0:T(8,128)(2,1)S(1)} %copy-done.75), kind=kOutput, calls=%fused_computation.104 | convolution fusion | flops 4834983936 | bytes 23592960 | tf_op jit(solution)/shard_map/dot_general | solution.py:12
  22.1 9.0 %fusion.70 = f32[256,3072]{1,0:T(8,128)S(1)} fusion(bf16[3072,3072]{1,0:T(8,128)(2,1)} %param.5, bf16[128,3072]{1,0:T(8,128)(2,1)S(1)} %collective-permute-done.4, bf16[128,3072]{1,0:T(8,128)(2,1)S(1)} %copy-done.74), kind=kOutput, calls=%fused_computation.88 | convolution fusion | flops 4834983936 | bytes 23592960 | tf_op jit(solution)/shard_map/dot_general | solution.py:12
  36.1 19.8 %collective-permute-done.33 = bf16[128,3072]{1,0:T(8,128)(2,1)S(1)} collective-permute-done((bf16[128,3072]{1,0:T(8,128)(2,1)S(1)}, bf16[128,3072]{1,0:T(8,128)(2,1)S(1)}, u32[]{:S(2)}, u32[]{:S(2)}) %collective-permute-start.33) | collective-permute-done | bytes 786464 | tf_op jit(solution)/shard_map/ppermute | solution.py:19
  63.9 9.2 %fusion.66 = f32[256,3072]{1,0:T(8,128)S(1)} fusion(bf16[3072,3072]{1,0:T(8,128)(2,1)} %param.5, bf16[128,3072]{1,0:T(8,128)(2,1)S(1)} %collective-permute-done.3, bf16[128,3072]{1,0:T(8,128)(2,1)} %collective-permute-done.2), kind=kOutput, calls=%fused_computation.84 | convolution fusion | flops 4834983936 | bytes 23592960 | tf_op jit(solution)/shard_map/dot_general | solution.py:12
  79.2 15.9 %collective-permute-done.5 = bf16[128,3072]{1,0:T(8,128)(2,1)S(1)} collective-permute-done((bf16[128,3072]{1,0:T(8,128)(2,1)S(1)}, bf16[128,3072]{1,0:T(8,128)(2,1)S(1)}, u32[]{:S(2)}, u32[]{:S(2)}) %collective-permute-start.5) | collective-permute-done | bytes 786464 | tf_op jit(solution)/shard_map/ppermute | solution.py:49
  104.2 10.4 %fusion.94 = f32[256,3072]{1,0:T(8,128)} fusion(bf16[3072,3072]{1,0:T(8,128)(2,1)} %param.6, bf16[128,3072]{1,0:T(8,128)(2,1)} %copy-done.80, bf16[128,3072]{1,0:T(8,128)(2,1)S(1)} %copy-done.79), kind=kOutput, calls=%fused_computation.112 | convolution fusion | flops 4834983936 | bytes 23592960 | tf_op jit(solution)/shard_map/dot_general | solution.py:12
  119.8 10.6 %fusion.102 = f32[256,3072]{1,0:T(8,128)} fusion(bf16[3072,3072]{1,0:T(8,128)(2,1)} %param.6, bf16[128,3072]{1,0:T(8,128)(2,1)} %collective-permute-done.42, bf16[128,3072]{1,0:T(8,128)(2,1)} %collective-permute-done.41), kind=kOutput, calls=%fused_computation.120 | convolution fusion | flops 4834983936 | bytes 23592960 | tf_op jit(solution)/shard_map/dot_general | solution.py:12
  132.2 11.3 %fusion.62 = f32[256,3072]{1,0:T(8,128)} fusion(bf16[3072,3072]{1,0:T(8,128)(2,1)} %param.5, bf16[128,3072]{1,0:T(8,128)(2,1)} %collective-permute-done.1, bf16[128,3072]{1,0:T(8,128)(2,1)} %collective-permute-done), kind=kOutput, calls=%fused_computation.80 | convolution fusion | flops 4834983936 | bytes 23592960 | tf_op jit(solution)/shard_map/dot_general | solution.py:12
  145.1 8.3 %fusion.78 = f32[256,3072]{1,0:T(8,128)} fusion(bf16[3072,3072]{1,0:T(8,128)(2,1)S(1)} %bitcast.21, bf16[128,3072]{1,0:T(8,128)(2,1)} %collective-permute-done.19, bf16[128,3072]{1,0:T(8,128)(2,1)} %collective-permute-done.18), kind=kOutput, calls=%fused_computation.96 | convolution fusion | flops 4834983936 | bytes 23592960 | tf_op jit(solution)/shard_map/dot_general | solution.py:12
  153.4 9.5 %fusion.110 = f32[256,3072]{1,0:T(8,128)S(1)} fusion(bf16[3072,3072]{1,0:T(8,128)(2,1)} %param.6, bf16[128,3072]{1,0:T(8,128)(2,1)} %collective-permute-done.49, bf16[128,3072]{1,0:T(8,128)(2,1)} %collective-permute-done.48), kind=kOutput, calls=%fused_computation.128 | convolution fusion | flops 4834983936 | bytes 23592960 | tf_op jit(solution)/shard_map/dot_general | solution.py:12
  199.0 8.1 %collective-permute-done.9 = bf16[128,3072]{1,0:T(8,128)(2,1)S(1)} collective-permute-done((bf16[128,3072]{1,0:T(8,128)(2,1)S(1)}, bf16[128,3072]{1,0:T(8,128)(2,1)S(1)}, u32[]{:S(2)}, u32[]{:S(2)}) %collective-permute-start.9) | collective-permute-done | bytes 786464 | tf_op jit(solution)/shard_map/ppermute | solution.py:52
  210.5 12.4 %collective-permute-done.15 = bf16[128,3072]{1,0:T(8,128)(2,1)S(1)} collective-permute-done((bf16[128,3072]{1,0:T(8,128)(2,1)S(1)}, bf16[128,3072]{1,0:T(8,128)(2,1)S(1)}, u32[]{:S(2)}, u32[]{:S(2)}) %collective-permute-start.15) | collective-permute-done | bytes 786464 | tf_op jit(solution)/shard_map/ppermute | solution.py:52
  240.7 9.0 %fusion.74 = f32[256,3072]{1,0:T(8,128)S(1)} fusion(bf16[3072,3072]{1,0:T(8,128)(2,1)} %param.6, bf16[128,3072]{1,0:T(8,128)(2,1)S(1)} %copy-done.84, bf16[128,3072]{1,0:T(8,128)(2,1)S(1)} %copy-done.82), kind=kOutput, calls=%fused_computation.92 | convolution fusion | flops 4834983936 | bytes 23592960 | tf_op jit(solution)/shard_map/dot_general | solution.py:12
  251.9 14.0 %collective-permute-done.20 = bf16[128,3072]{1,0:T(8,128)(2,1)S(1)} collective-permute-done((bf16[128,3072]{1,0:T(8,128)(2,1)S(1)}, bf16[128,3072]{1,0:T(8,128)(2,1)S(1)}, u32[]{:S(2)}, u32[]{:S(2)}) %collective-permute-start.20) | collective-permute-done | bytes 786464 | tf_op jit(solution)/shard_map/ppermute | solution.py:52
  288.8 9.4 %fusion.82 = f32[256,3072]{1,0:T(8,128)S(1)} fusion(bf16[3072,3072]{1,0:T(8,128)(2,1)} %param.6, bf16[128,3072]{1,0:T(8,128)(2,1)} %get-tuple-element.17, bf16[128,3072]{1,0:T(8,128)(2,1)} %get-tuple-element.20), kind=kOutput, calls=%fused_computation.100 | convolution fusion | flops 4834983936 | bytes 23592960 | tf_op jit(solution)/shard_map/dot_general | solution.py:12
  300.5 12.7 %collective-permute-done.28 = bf16[128,3072]{1,0:T(8,128)(2,1)S(1)} collective-permute-done((bf16[128,3072]{1,0:T(8,128)(2,1)}, bf16[128,3072]{1,0:T(8,128)(2,1)S(1)}, u32[]{:S(2)}, u32[]{:S(2)}) %collective-permute-start.28) | collective-permute-done | bytes 786464 | tf_op jit(solution)/shard_map/ppermute | solution.py:49
  315.1 6.1 collective-permute-done.29
  337.0 9.0 %fusion.90 = f32[256,3072]{1,0:T(8,128)S(1)} fusion(bf16[3072,3072]{1,0:T(8,128)(2,1)} %param.6, bf16[128,3072]{1,0:T(8,128)(2,1)S(1)} %copy-done.85, bf16[128,3072]{1,0:T(8,128)(2,1)S(1)} %copy-done.83), kind=kOutput, calls=%fused_computation.108 | convolution fusion | flops 4834983936 | bytes 23592960 | tf_op jit(solution)/shard_map/dot_general | solution.py:12
  348.3 15.0 %collective-permute-done.35 = bf16[128,3072]{1,0:T(8,128)(2,1)S(1)} collective-permute-done((bf16[128,3072]{1,0:T(8,128)(2,1)S(1)}, bf16[128,3072]{1,0:T(8,128)(2,1)S(1)}, u32[]{:S(2)}, u32[]{:S(2)}) %collective-permute-start.35) | collective-permute-done | bytes 786464 | tf_op jit(solution)/shard_map/ppermute | solution.py:52
  370.0 8.2 %collective-permute-done.38 = bf16[128,3072]{1,0:T(8,128)(2,1)S(1)} collective-permute-done((bf16[128,3072]{1,0:T(8,128)(2,1)S(1)}, bf16[128,3072]{1,0:T(8,128)(2,1)S(1)}, u32[]{:S(2)}, u32[]{:S(2)}) %collective-permute-start.38) | collective-permute-done | bytes 786464 | tf_op jit(solution)/shard_map/ppermute | solution.py:49
  388.4 6.3 collective-permute-start.44
  394.8 26.6 %multiply_convert_fusion = bf16[3072,3072]{1,0:T(8,128)(2,1)} fusion(bf16[1024,3072]{1,0:T(8,128)(2,1)} %get-tuple-element.4, bf16[1024,3072]{1,0:T(8,128)(2,1)} %constant_dynamic-update-slice_fusion.24), kind=kOutput, calls=%fused_computation | convolution fusion | flops 19346227200 | bytes 31457280 | tf_op jit(solution)/shard_map/dot_general | solution.py:113
  421.4 9.0 %fusion.98 = f32[256,3072]{1,0:T(8,128)S(1)} fusion(bf16[3072,3072]{1,0:T(8,128)(2,1)} %param.6, bf16[128,3072]{1,0:T(8,128)(2,1)S(1)} %get-tuple-element.5, bf16[128,3072]{1,0:T(8,128)(2,1)S(1)} %copy-done.72), kind=kOutput, calls=%fused_computation.116 | convolution fusion | flops 4834983936 | bytes 23592960 | tf_op jit(solution)/shard_map/dot_general | solution.py:12
  461.6 6.1 collective-permute-start.51
  467.7 10.6 %fusion.106 = f32[256,3072]{1,0:T(8,128)} fusion(bf16[3072,3072]{1,0:T(8,128)(2,1)} %param.5, bf16[128,3072]{1,0:T(8,128)(2,1)} %get-tuple-element.45, bf16[128,3072]{1,0:T(8,128)(2,1)} %get-tuple-element.48), kind=kOutput, calls=%fused_computation.124 | convolution fusion | flops 4834983936 | bytes 23592960 | tf_op jit(solution)/shard_map/dot_general | solution.py:12
  511.7 9.5 %fusion.114 = f32[256,3072]{1,0:T(8,128)S(1)} fusion(bf16[3072,3072]{1,0:T(8,128)(2,1)} %param.5, bf16[128,3072]{1,0:T(8,128)(2,1)} %get-tuple-element.39, bf16[128,3072]{1,0:T(8,128)(2,1)} %get-tuple-element.42), kind=kOutput, calls=%fused_computation.132 | convolution fusion | flops 4834983936 | bytes 23592960 | tf_op jit(solution)/shard_map/dot_general | solution.py:12
  526.4 11.0 %collective-permute-done.56 = bf16[128,3072]{1,0:T(8,128)(2,1)S(1)} collective-permute-done((bf16[128,3072]{1,0:T(8,128)(2,1)}, bf16[128,3072]{1,0:T(8,128)(2,1)S(1)}, u32[]{:S(2)}, u32[]{:S(2)}) %collective-permute-start.56) | collective-permute-done | bytes 786464 | tf_op jit(solution)/shard_map/ppermute | solution.py:52
  554.3 9.0 %fusion.118 = f32[256,3072]{1,0:T(8,128)S(1)} fusion(bf16[3072,3072]{1,0:T(8,128)(2,1)} %param.5, bf16[128,3072]{1,0:T(8,128)(2,1)S(1)} %copy-done.73, bf16[128,3072]{1,0:T(8,128)(2,1)S(1)} %copy-done.71), kind=kOutput, calls=%fused_computation.136 | convolution fusion | flops 4834983936 | bytes 23592960 | tf_op jit(solution)/shard_map/dot_general | solution.py:12
  564.6 17.2 %collective-permute-done.62 = bf16[128,3072]{1,0:T(8,128)(2,1)} collective-permute-done((bf16[128,3072]{1,0:T(8,128)(2,1)}, bf16[128,3072]{1,0:T(8,128)(2,1)}, u32[]{:S(2)}, u32[]{:S(2)}) %collective-permute-start.62) | collective-permute-done | bytes 786464 | tf_op jit(solution)/shard_map/ppermute | solution.py:52
  590.8 9.5 %fusion.122 = f32[256,3072]{1,0:T(8,128)S(1)} fusion(bf16[3072,3072]{1,0:T(8,128)(2,1)} %param.5, bf16[128,3072]{1,0:T(8,128)(2,1)} %get-tuple-element.29, bf16[128,3072]{1,0:T(8,128)(2,1)} %get-tuple-element.31), kind=kOutput, calls=%fused_computation.140 | convolution fusion | flops 4834983936 | bytes 23592960 | tf_op jit(solution)/shard_map/dot_general | solution.py:12
  603.4 10.5 %collective-permute-done.40 = bf16[128,3072]{1,0:T(8,128)(2,1)S(1)} collective-permute-done((bf16[128,3072]{1,0:T(8,128)(2,1)}, bf16[128,3072]{1,0:T(8,128)(2,1)S(1)}, u32[]{:S(2)}, u32[]{:S(2)}) %collective-permute-start.40) | collective-permute-done | bytes 786464 | tf_op jit(solution)/shard_map/ppermute | solution.py:19
  622.7 26.9 %multiply_convert_fusion.1 = bf16[3072,3072]{1,0:T(8,128)(2,1)} fusion(bf16[1024,3072]{1,0:T(8,128)(2,1)} %constant_dynamic-update-slice_fusion, bf16[1024,3072]{1,0:T(8,128)(2,1)} %get-tuple-element.28), kind=kOutput, calls=%fused_computation.1 | convolution fusion | flops 19346227200 | bytes 31457280 | tf_op jit(solution)/shard_map/dot_general | solution.py:113
  (383 shorter events, 279.9 us)
Async XLA Ops:
  4.2 53.0 %collective-permute-start = (bf16[128,3072]{1,0:T(8,128)(2,1)}, bf16[128,3072]{1,0:T(8,128)(2,1)}, u32[]{:S(2)}, u32[]{:S(2)}) collective-permute-start(bf16[128,3072]{1,0:T(8,128)(2,1)} %param.4), channel_id=1, source_target_pairs={{0,4},{1,5},{2,6},{3,7},{4,0},{5,1},{6,2},{7,3},{8,12},{9,13},{10,... | collective-permute-start | bytes 2359304 | tf_op jit(solution)/shard_map/ppermute | solution.py:19
  5.7 55.2 %collective-permute-start.18 = (bf16[128,3072]{1,0:T(8,128)(2,1)}, bf16[128,3072]{1,0:T(8,128)(2,1)}, u32[]{:S(2)}, u32[]{:S(2)}) collective-permute-start(bf16[128,3072]{1,0:T(8,128)(2,1)} %param.4), channel_id=1, source_target_pairs={{0,6},{1,7},{2,4},{3,5},{4,2},{5,3},{6,0},{7,1},{8,14},{9,15},{10,... | collective-permute-start | bytes 2359304 | tf_op jit(solution)/shard_map/ppermute | solution.py:19
  7.9 48.0 %collective-permute-start.33 = (bf16[128,3072]{1,0:T(8,128)(2,1)S(1)}, bf16[128,3072]{1,0:T(8,128)(2,1)S(1)}, u32[]{:S(2)}, u32[]{:S(2)}) collective-permute-start(bf16[128,3072]{1,0:T(8,128)(2,1)S(1)} %copy-done.75), channel_id=1, source_target_pairs={{0,2},{1,3},{2,0},{3,1},{4,6},{5,7},{6,4},{7,5},{8,10},{9,11},{10,... | collective-permute-start | bytes 2359304 | tf_op jit(solution)/shard_map/ppermute | solution.py:19
  20.6 41.0 %collective-permute-start.41 = (bf16[128,3072]{1,0:T(8,128)(2,1)S(1)}, bf16[128,3072]{1,0:T(8,128)(2,1)}, u32[]{:S(2)}, u32[]{:S(2)}) collective-permute-start(bf16[128,3072]{1,0:T(8,128)(2,1)S(1)} %copy-done.75), channel_id=1, source_target_pairs={{0,4},{1,5},{2,6},{3,7},{4,0},{5,1},{6,2},{7,3},{8,12},{9,13},{10,... | collective-permute-start | bytes 2359304 | tf_op jit(solution)/shard_map/ppermute | solution.py:19
  32.2 41.9 %collective-permute-start.48 = (bf16[128,3072]{1,0:T(8,128)(2,1)S(1)}, bf16[128,3072]{1,0:T(8,128)(2,1)}, u32[]{:S(2)}, u32[]{:S(2)}) collective-permute-start(bf16[128,3072]{1,0:T(8,128)(2,1)S(1)} %copy-done.75), channel_id=1, source_target_pairs={{0,6},{1,7},{2,4},{3,5},{4,2},{5,3},{6,0},{7,1},{8,14},{9,15},{10,... | collective-permute-start | bytes 2359304 | tf_op jit(solution)/shard_map/ppermute | solution.py:19
  61.6 33.5 %collective-permute-start.5 = (bf16[128,3072]{1,0:T(8,128)(2,1)S(1)}, bf16[128,3072]{1,0:T(8,128)(2,1)S(1)}, u32[]{:S(2)}, u32[]{:S(2)}) collective-permute-start(bf16[128,3072]{1,0:T(8,128)(2,1)S(1)} %get-tuple-element.110), channel_id=1, source_target_pairs={{0,8},{1,9},{2,10},{3,11},{4,12},{5,13},{6,14},{7,15}} | collective-permute-start | bytes 2359304 | tf_op jit(solution)/shard_map/ppermute | solution.py:49
  78.7 51.8 %collective-permute-start.1 = (bf16[128,3072]{1,0:T(8,128)(2,1)}, bf16[128,3072]{1,0:T(8,128)(2,1)}, u32[]{:S(2)}, u32[]{:S(2)}) collective-permute-start(bf16[128,3072]{1,0:T(8,128)(2,1)} %collective-permute-done), channel_id=1, source_target_pairs={{0,1},{1,0},{2,3},{3,2},{4,5},{5,4},{6,7},{7,6},{8,9},{9,8},{10,11... | collective-permute-start | bytes 2359304 | tf_op jit(solution)/shard_map/ppermute | solution.py:19
  78.7 64.8 %collective-permute-start.19 = (bf16[128,3072]{1,0:T(8,128)(2,1)}, bf16[128,3072]{1,0:T(8,128)(2,1)}, u32[]{:S(2)}, u32[]{:S(2)}) collective-permute-start(bf16[128,3072]{1,0:T(8,128)(2,1)} %collective-permute-done.18), channel_id=1, source_target_pairs={{0,1},{1,0},{2,3},{3,2},{4,5},{5,4},{6,7},{7,6},{8,9},{9,8},{10,11... | collective-permute-start | bytes 2359304 | tf_op jit(solution)/shard_map/ppermute | solution.py:19
  95.1 58.3 %collective-permute-start.49 = (bf16[128,3072]{1,0:T(8,128)(2,1)}, bf16[128,3072]{1,0:T(8,128)(2,1)}, u32[]{:S(2)}, u32[]{:S(2)}) collective-permute-start(bf16[128,3072]{1,0:T(8,128)(2,1)} %collective-permute-done.48), channel_id=1, source_target_pairs={{0,1},{1,0},{2,3},{3,2},{4,5},{5,4},{6,7},{7,6},{8,9},{9,8},{10,11... | collective-permute-start | bytes 2359304 | tf_op jit(solution)/shard_map/ppermute | solution.py:19
  99.8 81.0 %collective-permute-start.7 = (bf16[128,3072]{1,0:T(8,128)(2,1)}, bf16[128,3072]{1,0:T(8,128)(2,1)S(1)}, u32[]{:S(2)}, u32[]{:S(2)}) collective-permute-start(bf16[128,3072]{1,0:T(8,128)(2,1)} %broadcast_select_fusion.48), channel_id=1, source_target_pairs={{0,8},{8,16},{1,9},{9,17},{2,10},{10,18},{3,11},{11,19},{4,12},{12... | collective-permute-start | bytes 2359304 | tf_op jit(solution)/shard_map/ppermute | solution.py:49
  115.7 65.1 %collective-permute-start.13 = (bf16[128,3072]{1,0:T(8,128)(2,1)}, bf16[128,3072]{1,0:T(8,128)(2,1)S(1)}, u32[]{:S(2)}, u32[]{:S(2)}) collective-permute-start(bf16[128,3072]{1,0:T(8,128)(2,1)} %broadcast_select_fusion.39), channel_id=1, source_target_pairs={{0,8},{8,16},{1,9},{9,17},{2,10},{10,18},{3,11},{11,19},{4,12},{12... | collective-permute-start | bytes 2359304 | tf_op jit(solution)/shard_map/ppermute | solution.py:49
  130.5 50.3 %collective-permute-start.14 = (bf16[128,3072]{1,0:T(8,128)(2,1)}, bf16[128,3072]{1,0:T(8,128)(2,1)}, u32[]{:S(2)}, u32[]{:S(2)}) collective-permute-start(bf16[128,3072]{1,0:T(8,128)(2,1)} %get-tuple-element.86), channel_id=1, source_target_pairs={{24,16},{16,8},{25,17},{17,9},{26,18},{18,10},{27,19},{19,11},{28,... | collective-permute-start | bytes 2359304 | tf_op jit(solution)/shard_map/ppermute | solution.py:52
  143.5 37.3 %collective-permute-start.8 = (bf16[128,3072]{1,0:T(8,128)(2,1)}, bf16[128,3072]{1,0:T(8,128)(2,1)}, u32[]{:S(2)}, u32[]{:S(2)}) collective-permute-start(bf16[128,3072]{1,0:T(8,128)(2,1)} %get-tuple-element.101), channel_id=1, source_target_pairs={{24,16},{16,8},{25,17},{17,9},{26,18},{18,10},{27,19},{19,11},{28,... | collective-permute-start | bytes 2359304 | tf_op jit(solution)/shard_map/ppermute | solution.py:52
  228.2 39.6 %collective-permute-start.22 = (bf16[128,3072]{1,0:T(8,128)(2,1)S(1)}, bf16[128,3072]{1,0:T(8,128)(2,1)S(1)}, u32[]{:S(2)}, u32[]{:S(2)}) collective-permute-start(bf16[128,3072]{1,0:T(8,128)(2,1)S(1)} %broadcast_select_fusion.30), channel_id=1, source_target_pairs={{24,16},{16,8},{8,0},{25,17},{17,9},{9,1},{26,18},{18,10},{10,2},{... | collective-permute-start | bytes 2359304 | tf_op jit(solution)/shard_map/ppermute | solution.py:52
  229.6 36.3 %collective-permute-start.20 = (bf16[128,3072]{1,0:T(8,128)(2,1)S(1)}, bf16[128,3072]{1,0:T(8,128)(2,1)S(1)}, u32[]{:S(2)}, u32[]{:S(2)}) collective-permute-start(bf16[128,3072]{1,0:T(8,128)(2,1)S(1)} %broadcast_select_fusion.33), channel_id=1, source_target_pairs={{24,16},{16,8},{8,0},{25,17},{17,9},{9,1},{26,18},{18,10},{10,2},{... | collective-permute-start | bytes 2359304 | tf_op jit(solution)/shard_map/ppermute | solution.py:52
  231.1 34.8 %collective-permute-start.21 = (bf16[128,3072]{1,0:T(8,128)(2,1)S(1)}, bf16[128,3072]{1,0:T(8,128)(2,1)S(1)}, u32[]{:S(2)}, u32[]{:S(2)}) collective-permute-start(bf16[128,3072]{1,0:T(8,128)(2,1)S(1)} %get-tuple-element.96), channel_id=1, source_target_pairs={{0,8},{8,16},{16,24},{1,9},{9,17},{17,25},{2,10},{10,18},{18,26},{... | collective-permute-start | bytes 2359304 | tf_op jit(solution)/shard_map/ppermute | solution.py:49
  236.8 32.5 %collective-permute-start.23 = (bf16[128,3072]{1,0:T(8,128)(2,1)S(1)}, bf16[128,3072]{1,0:T(8,128)(2,1)S(1)}, u32[]{:S(2)}, u32[]{:S(2)}) collective-permute-start(bf16[128,3072]{1,0:T(8,128)(2,1)S(1)} %get-tuple-element.76), channel_id=1, source_target_pairs={{0,8},{8,16},{16,24},{1,9},{9,17},{17,25},{2,10},{10,18},{18,26},{... | collective-permute-start | bytes 2359304 | tf_op jit(solution)/shard_map/ppermute | solution.py:49
  251.9 348.5 %collective-permute-start.17 = (f32[128,3072]{1,0:T(8,128)}, f32[128,3072]{1,0:T(8,128)}, u32[]{:S(2)}, u32[]{:S(2)}) collective-permute-start(f32[128,3072]{1,0:T(8,128)} %slice.135), channel_id=1, source_target_pairs={{0,1},{1,0},{2,3},{3,2},{4,5},{5,4},{6,7},{7,6},{8,9},{9,8},{10,11... | collective-permute-start | bytes 4718600 | tf_op jit(solution)/shard_map/ppermute | solution.py:19
  276.8 38.2 %collective-permute-start.30 = (bf16[128,3072]{1,0:T(8,128)(2,1)}, bf16[128,3072]{1,0:T(8,128)(2,1)S(1)}, u32[]{:S(2)}, u32[]{:S(2)}) collective-permute-start(bf16[128,3072]{1,0:T(8,128)(2,1)} %broadcast_select_fusion.23), channel_id=1, source_target_pairs={{0,8},{8,16},{16,24},{1,9},{9,17},{17,25},{2,10},{10,18},{18,26},{... | collective-permute-start | bytes 2359304 | tf_op jit(solution)/shard_map/ppermute | solution.py:49
  287.3 33.9 %collective-permute-start.29 = (bf16[128,3072]{1,0:T(8,128)(2,1)S(1)}, bf16[128,3072]{1,0:T(8,128)(2,1)S(1)}, u32[]{:S(2)}, u32[]{:S(2)}) collective-permute-start(bf16[128,3072]{1,0:T(8,128)(2,1)S(1)} %copy-done.68), channel_id=1, source_target_pairs={{24,16},{16,8},{8,0},{25,17},{17,9},{9,1},{26,18},{18,10},{10,2},{... | collective-permute-start | bytes 2359304 | tf_op jit(solution)/shard_map/ppermute | solution.py:52
  313.2 120.1 %collective-permute-start.24 = (f32[128,3072]{1,0:T(8,128)}, f32[128,3072]{1,0:T(8,128)}, u32[]{:S(2)}, u32[]{:S(2)}) collective-permute-start(f32[128,3072]{1,0:T(8,128)} %slice.139), channel_id=1, source_target_pairs={{0,1},{1,0},{2,3},{3,2},{4,5},{5,4},{6,7},{7,6},{8,9},{9,8},{10,11... | collective-permute-start | bytes 4718600 | tf_op jit(solution)/shard_map/ppermute | solution.py:19
  328.8 41.2 %collective-permute-start.37 = (bf16[128,3072]{1,0:T(8,128)(2,1)}, bf16[128,3072]{1,0:T(8,128)(2,1)S(1)}, u32[]{:S(2)}, u32[]{:S(2)}) collective-permute-start(bf16[128,3072]{1,0:T(8,128)(2,1)} %broadcast_select_fusion.19), channel_id=1, source_target_pairs={{24,16},{16,8},{8,0},{25,17},{17,9},{9,1},{26,18},{18,10},{10,2},{... | collective-permute-start | bytes 2359304 | tf_op jit(solution)/shard_map/ppermute | solution.py:52
  330.3 33.0 %collective-permute-start.35 = (bf16[128,3072]{1,0:T(8,128)(2,1)S(1)}, bf16[128,3072]{1,0:T(8,128)(2,1)S(1)}, u32[]{:S(2)}, u32[]{:S(2)}) collective-permute-start(bf16[128,3072]{1,0:T(8,128)(2,1)S(1)} %broadcast_select_fusion.21), channel_id=1, source_target_pairs={{24,16},{16,8},{8,0},{25,17},{17,9},{9,1},{26,18},{18,10},{10,2},{... | collective-permute-start | bytes 2359304 | tf_op jit(solution)/shard_map/ppermute | solution.py:52
  331.8 34.7 %collective-permute-start.36 = (bf16[128,3072]{1,0:T(8,128)(2,1)S(1)}, bf16[128,3072]{1,0:T(8,128)(2,1)S(1)}, u32[]{:S(2)}, u32[]{:S(2)}) collective-permute-start(bf16[128,3072]{1,0:T(8,128)(2,1)S(1)} %copy-done.70), channel_id=1, source_target_pairs={{0,8},{8,16},{16,24},{1,9},{9,17},{17,25},{2,10},{10,18},{18,26},{... | collective-permute-start | bytes 2359304 | tf_op jit(solution)/shard_map/ppermute | solution.py:49
  366.4 115.4 %collective-permute-start.31 = (f32[128,3072]{1,0:T(8,128)}, f32[128,3072]{1,0:T(8,128)}, u32[]{:S(2)}, u32[]{:S(2)}) collective-permute-start(f32[128,3072]{1,0:T(8,128)} %slice.143), channel_id=1, source_target_pairs={{0,1},{1,0},{2,3},{3,2},{4,5},{5,4},{6,7},{7,6},{8,9},{9,8},{10,11... | collective-permute-start | bytes 4718600 | tf_op jit(solution)/shard_map/ppermute | solution.py:19
  387.2 50.2 %collective-permute-start.43 = (bf16[128,3072]{1,0:T(8,128)(2,1)}, bf16[128,3072]{1,0:T(8,128)(2,1)S(1)}, u32[]{:S(2)}, u32[]{:S(2)}) collective-permute-start(bf16[128,3072]{1,0:T(8,128)(2,1)} %broadcast_select_fusion.17), channel_id=1, source_target_pairs={{24,16},{16,8},{8,0},{25,17},{17,9},{9,1},{26,18},{18,10},{10,2},{... | collective-permute-start | bytes 2359304 | tf_op jit(solution)/shard_map/ppermute | solution.py:52
  388.4 53.7 %collective-permute-start.44 = (bf16[128,3072]{1,0:T(8,128)(2,1)}, bf16[128,3072]{1,0:T(8,128)(2,1)}, u32[]{:S(2)}, u32[]{:S(2)}) collective-permute-start(bf16[128,3072]{1,0:T(8,128)(2,1)} %get-tuple-element.90), channel_id=1, source_target_pairs={{0,8},{8,16},{16,24},{1,9},{9,17},{17,25},{2,10},{10,18},{18,26},{... | collective-permute-start | bytes 2359304 | tf_op jit(solution)/shard_map/ppermute | solution.py:49
  442.2 80.4 %collective-permute-start.39 = (f32[128,3072]{1,0:T(8,128)}, f32[128,3072]{1,0:T(8,128)}, u32[]{:S(2)}, u32[]{:S(2)}) collective-permute-start(f32[128,3072]{1,0:T(8,128)} %slice.147), channel_id=1, source_target_pairs={{0,1},{1,0},{2,3},{3,2},{4,5},{5,4},{6,7},{7,6},{8,9},{9,8},{10,11... | collective-permute-start | bytes 4718600 | tf_op jit(solution)/shard_map/ppermute | solution.py:19
  506.6 35.5 %collective-permute-start.58 = (bf16[128,3072]{1,0:T(8,128)(2,1)}, bf16[128,3072]{1,0:T(8,128)(2,1)S(1)}, u32[]{:S(2)}, u32[]{:S(2)}) collective-permute-start(bf16[128,3072]{1,0:T(8,128)(2,1)} %broadcast_select_fusion.5), channel_id=1, source_target_pairs={{16,8},{8,0},{17,9},{9,1},{18,10},{10,2},{19,11},{11,3},{20,12},{1... | collective-permute-start | bytes 2359304 | tf_op jit(solution)/shard_map/ppermute | solution.py:52
  548.1 39.5 %collective-permute-start.64 = (bf16[128,3072]{1,0:T(8,128)(2,1)S(1)}, bf16[128,3072]{1,0:T(8,128)(2,1)}, u32[]{:S(2)}, u32[]{:S(2)}) collective-permute-start(bf16[128,3072]{1,0:T(8,128)(2,1)S(1)} %broadcast_select_fusion.1), channel_id=1, source_target_pairs={{8,0},{9,1},{10,2},{11,3},{12,4},{13,5},{14,6},{15,7}} | collective-permute-start | bytes 2359304 | tf_op jit(solution)/shard_map/ppermute | solution.py:52
  553.6 34.0 %collective-permute-start.65 = (bf16[128,3072]{1,0:T(8,128)(2,1)}, bf16[128,3072]{1,0:T(8,128)(2,1)S(1)}, u32[]{:S(2)}, u32[]{:S(2)}) collective-permute-start(bf16[128,3072]{1,0:T(8,128)(2,1)} %get-tuple-element.56), channel_id=1, source_target_pairs={{16,24},{17,25},{18,26},{19,27},{20,28},{21,29},{22,30},{23,31}} | collective-permute-start | bytes 2359304 | tf_op jit(solution)/shard_map/ppermute | solution.py:49
  600.4 49.2 %collective-permute-start.47 = (f32[128,3072]{1,0:T(8,128)}, f32[128,3072]{1,0:T(8,128)S(1)}, u32[]{:S(2)}, u32[]{:S(2)}) collective-permute-start(f32[128,3072]{1,0:T(8,128)} %slice.151), channel_id=1, source_target_pairs={{0,1},{1,0},{2,3},{3,2},{4,5},{5,4},{6,7},{7,6},{8,9},{9,8},{10,11... | collective-permute-start | bytes 4718600 | tf_op jit(solution)/shard_map/ppermute | solution.py:19
  (128 other events, 1551.6 us)
